TPU v7x, 256 devices: a whole 4x4x8 slice. The times are simulated.
256 devices in a mesh: row: 64 (over z, y, core), col: 4 (over x).
Axes of the slice: x: 4, y: 4, z: 8, core: 2. Of those that a mesh axis runs over, the one named last changes fastest.
Arguments:
- row_embed: float32 [65536, 512], P(('row', 'col')), may hold values from -1.5 to 1.5
- row_accum: float32 [65536, 512], P(('row', 'col')), may hold values from 0.001 to 0.01
- col_embed: float32 [4, 4096, 512], P('col', 'row'), may hold values from -1.5 to 1.5
- col_accum: float32 [4, 4096, 512], P('col', 'row'), may hold values from 0.001 to 0.01
- col_freq: int32 [4, 4096], P('col'), may hold values from 1000 to 29999
- row_freq: int32 [65536], P('row'), may hold values from 1000 to 29999
- block_cols: int32 [64, 4, 2], P('row', 'col'), may hold values from 0 to 3, all different within a row
- counts: int32 [64, 4, 2, 1024, 1024], P('row', 'col'), may hold values from 0 to 1024
- excluded: int32 [512], replicated, may hold values from 0 to 65535
- log_total: float32 [], replicated, may hold values from 15 to 19
Outputs:
- row_embed_new: float32 [65536, 512], P(('row', 'col'))
- row_accum_new: float32 [65536, 512], P(('row', 'col'))
- col_embed_new: float32 [4, 4096, 512], P('col', 'row')
- col_accum_new: float32 [4, 4096, 512], P('col', 'row')
Inputs may be any that keep to these rules, and one draw needn't show every extreme that they name: `block_cols`: the 2 column blocks of one row block and group are different.
All inputs are finite; a program needn't handle non-finite values.
Results may differ from a plain program's by a relative error of at most 0.0071.
The roundings to bfloat16 on the way count: a program that leaves them out, or rounds other values in their place, can miss the bound.
Values may be sent and summed in bfloat16 or wider, within the bound.
A program may use at most 128 MiB of HBM per device.

v0:
```python
import jax
import jax.numpy as jnp
from jax import lax
from jax.experimental import pallas as pl
from jax.experimental.pallas import tpu as pltpu
from jax.sharding import PartitionSpec as P

MESH = pl.DeviceIdType.MESH
NX, NY, NZ, NK = 4, 4, 8, 2
BLOCK = 1024
HALF = 512
EXCLUDED = 512
PIECE = 64
QUARTER = 256
D = 512
F32 = jnp.float32
BF16 = jnp.bfloat16

learn_rate = 0.2
decay_rate = 0.5

GATHER_ORDER = (1, 7, 3, 5, 0, 2, 6, 4)
REDUCE_ORDER = (3, 5, 1, 7, 4, 2, 6, 0)
OWN_IN = GATHER_ORDER.index(0)
OWN_OUT = REDUCE_ORDER.index(0)
FIRST = GATHER_ORDER[1] % 2
OTHERS = tuple(j for j in range(NZ) if j != OWN_OUT)

GATHER_MORE = 1
GATHER_NEAR = 2
GATHER_FAR = 4
CELLS = 8
REDUCE = 10
CELLS_MORE = REDUCE + 2
REDUCE_FAR = REDUCE + 2
REDUCE_NEAR = REDUCE + 4
REDUCE_HOME = REDUCE + 6
ROWS = REDUCE + 5


def pick(index, values):
    result = jnp.int32(values[-1])
    for place in range(len(values) - 1):
        result = jnp.where(index == place, jnp.int32(values[place]), result)
    return result


def step_kernel(
    chosen, total, row_in, col_in, row_freq_in, col_freq_in, excluded_in, row_accum, col_accum, counts,
    result,
    row_local, col_local, row_freq, col_freq, excluded,
    made, own_grad, col_grad, row_sums, col_sums, decay,
    cols, mine, rows, cnt, wgt, base, cells, row_logs,
    part, pair_in, send_half, recv_half, send_full, recv_full, send_z, recv_z,
    xsend_half, xrecv_half, xsend_full, xrecv_full,
    cnt_sem, ag_s, ag_r, rs_s, rs_r, x_s, x_r,
):
    r = lax.axis_index("row")
    x = lax.axis_index("col")
    k = lax.rem(r, NK)
    y = lax.rem(r // NK, NY)
    z = r // (NK * NY)
    yp, ym, y2 = lax.rem(y + 1, NY), lax.rem(y + 3, NY), lax.rem(y + 2, NY)
    xp, xm, x2 = lax.rem(x + 1, NX), lax.rem(x + 3, NX), lax.rem(x + 2, NX)
    other = 1 - k

    def dev(dx, dy, dz, dk):
        return ((dz * NY + dy) * NK + dk, dx)

    right, left = dev(x, yp, z, k), dev(x, ym, z, k)
    east, west = dev(xp, y, z, k), dev(xm, y, z, k)
    mate = dev(x, y, z, other)

    def remote(src, dst, s, q, target):
        return pltpu.make_async_remote_copy(
            src_ref=src, dst_ref=dst, send_sem=s, recv_sem=q, device_id=target, device_id_type=MESH
        )

    def count_copy(c):
        h, s, b = c // 4, (c // 2) % 2, c % 2
        lane = pl.multiple_of(lax.rem(z + h + FIRST, 2) * HALF, HALF)
        return pltpu.make_async_copy(
            counts.at[s, pl.ds(b * HALF, HALF), pl.ds(lane, HALF)],
            cnt.at[s, h, pl.ds(b * HALF, HALF)],
            cnt_sem.at[c],
        )

    def sums_copy(i):
        return pltpu.make_async_copy(
            (row_accum, col_accum)[i], (row_sums, col_sums)[i], cnt_sem.at[8 + i]
        )

    barrier = pltpu.get_barrier_semaphore()
    for target in (right, left, east, west, mate):
        pl.semaphore_signal(barrier, inc=1, device_id=target, device_id_type=MESH)
    for dz in range(1, NZ):
        pl.semaphore_signal(
            barrier, inc=1, device_id=dev(x, y, lax.rem(z + dz, NZ), k), device_id_type=MESH
        )
    sources = (col_in, row_in, row_freq_in, col_freq_in, excluded_in)
    targets = (col_local, row_local, row_freq, col_freq, excluded)
    for i in range(5):
        pltpu.make_async_copy(sources[i], targets[i], cnt_sem.at[12 + i]).start()

    for c in range(8):
        count_copy(c).start()
    for i in range(2):
        sums_copy(i).start()

    def ready(i):
        pltpu.make_async_copy(sources[i], targets[i], cnt_sem.at[12 + i]).wait()

    ready(0)
    cols[z, y, k] = col_local[...].astype(BF16)
    my_rows = pl.multiple_of(x * QUARTER, QUARTER)
    ready(1)
    rows[pl.ds(my_rows, QUARTER)] = row_local[...].astype(BF16)
    pl.semaphore_wait(barrier, 5 + NZ - 1)

    def z_copy(i):
        zt = lax.rem(z + pick(i, GATHER_ORDER), NZ)
        return remote(cols.at[z, y, k], cols.at[z, y, k], ag_s.at[0, i], ag_r.at[0, z], dev(x, y, zt, k))

    def z_arrival(zs):
        return remote(cols.at[zs, y, k], cols.at[zs, y, k], ag_s.at[0, 0], ag_r.at[0, zs], mate)

    def y_copy(zs, up):
        kind, target = (1, right) if up else (2, left)
        return remote(cols.at[zs, y, k], cols.at[zs, y, k], ag_s.at[kind, zs], ag_r.at[kind, zs], target)

    def y_arrival(zs, up):
        kind, src = (1, ym) if up else (2, yp)
        return remote(cols.at[zs, src, k], cols.at[zs, src, k], ag_s.at[kind, zs], ag_r.at[kind, zs], mate)

    def y_forward(zs, up):
        kind, src, start, target = (3, ym, 0, right) if up else (4, yp, PIECE // 2, left)
        ref = cols.at[zs, src, k, pl.ds(start, PIECE // 2)]
        return remote(ref, ref, ag_s.at[kind, zs], ag_r.at[kind, zs], target)

    def y_far(zs, up):
        kind, start = (3, 0) if up else (4, PIECE // 2)
        ref = cols.at[zs, y2, k, pl.ds(start, PIECE // 2)]
        return remote(ref, ref, ag_s.at[kind, zs], ag_r.at[kind, zs], mate)

    def mate_copy(zs):
        return remote(cols.at[zs, :, k], cols.at[zs, :, k], ag_s.at[5, zs], ag_r.at[5, zs], mate)

    def mate_arrival(zs):
        return remote(cols.at[zs, :, other], cols.at[zs, :, other], ag_s.at[5, zs], ag_r.at[5, zs], mate)

    def quarter(q, start, size):
        return rows.at[pl.ds(pl.multiple_of(q * QUARTER + start, 128), size)]

    def x_copy(i):
        n = 128
        q, start, target = ((x, 0, east), (x, n, west), (x, n, east), (x, 0, west), (xm, 0, east), (xp, n, west))[i]
        return remote(quarter(q, start, n), quarter(q, start, n), x_s.at[i], x_r.at[i], target)

    def x_arrival(i):
        n = 128
        q, start = ((xm, 0), (xp, n), (xm, n), (xp, 0), (x2, 0), (x2, n))[i]
        return remote(quarter(q, start, n), quarter(q, start, n), x_s.at[i], x_r.at[i], mate)

    y_copy(z, True).start()
    y_copy(z, False).start()
    for i in range(4):
        if i != OWN_IN:
            z_copy(i).start()
    for i in range(4):
        x_copy(i).start()

    for i in range(2, 5):
        ready(i)
    logs = jnp.log(row_freq[...].astype(F32)) - total[0]
    row_logs[...] = jnp.broadcast_to(logs, (128, BLOCK)).T

    ids = r * BLOCK + my_rows + lax.broadcasted_iota(jnp.int32, (QUARTER, EXCLUDED), 0)
    listed = jnp.max(jnp.where(ids == excluded[...], 1.0, 0.0), axis=1, keepdims=True)
    root = jnp.sqrt(row_freq[:, pl.ds(my_rows, QUARTER)].astype(F32))
    coef = jnp.broadcast_to(decay_rate * root / (root + 30.0), (128, QUARTER)).T
    decay[...] = jnp.where(listed > 0.0, 0.0, coef)

    def of_block(block, options):
        result = options[3]
        for b in range(3):
            result = lax.select(block == b, options[b], result)
        return result

    def prepare(c):
        h, s = c // 4, lax.rem(c // 2, 2)
        first = lax.rem(c, 2) * HALF
        ref = cnt.at[s, h, pl.ds(first, HALF)]
        pltpu.make_async_copy(ref, ref, cnt_sem.at[c]).wait()
        parity = lax.rem(z + h + FIRST, 2)
        freq = of_block(
            chosen[s],
            [col_freq[:, pl.ds(pl.multiple_of(b * BLOCK + parity * HALF, HALF), HALF)] for b in range(4)],
        )
        col_logs = jnp.log(freq.astype(F32))

        def tile(n, _):
            at = pl.ds(pl.multiple_of(first + n * PIECE, PIECE), PIECE)
            rl = row_logs[at]
            for lane in range(0, HALF, 128):
                count = cnt[s, h, at, lane : lane + 128]
                full = count > 0
                value = jnp.maximum(count, 1).astype(F32)
                root = value * lax.rsqrt(value)
                base[s, h, at, lane : lane + 128] = (rl + col_logs[:, lane : lane + 128]) - jnp.log(value)
                wgt[s, h, at, lane : lane + 128] = jnp.where(
                    full, (0.1 / BLOCK) + (0.25 / BLOCK) * root, 0.0
                )
            return 0

        lax.fori_loop(0, HALF // PIECE, tile, 0)

    def cell_tile(h, n):
        s, q = n // 2, lax.rem(n, 2)
        parity = lax.rem(z + h + FIRST, 2)
        col_tile = of_block(
            chosen[s], [cols[2 * b + parity, pl.ds(2 * q, 2)].reshape(QUARTER, D) for b in range(4)]
        )
        mine[s, h, q] = col_tile
        lane = pl.multiple_of(q * QUARTER, QUARTER)
        for m in range(4):
            at = pl.ds(m * QUARTER, QUARTER)
            predicted = lax.dot_general(
                rows[at], col_tile, (((1,), (1,)), ((), ())), preferred_element_type=F32
            )
            shifted = predicted + base[s, h, at, pl.ds(lane, QUARTER)]
            w = wgt[s, h, at, pl.ds(lane, QUARTER)]
            hinge = 1.0 / (BLOCK + BLOCK * jnp.exp(-shifted))
            cells[s, h, at, pl.ds(lane, QUARTER)] = jnp.where(w > 0.0, w * shifted, hinge).astype(BF16)

    def mate_send(i):
        return remote(part.at[i, :, other], pair_in.at[i], rs_s.at[0, i], rs_r.at[0, i], mate)

    def mate_recv(i):
        return remote(pair_in.at[i], pair_in.at[i], rs_s.at[0, i], rs_r.at[0, i], mate)

    def half_copy(i, up):
        n, target = (0, right) if up else (1, left)
        return remote(send_half.at[n, i], recv_half.at[n, i], rs_s.at[1 + n, i], rs_r.at[1 + n, i], target)

    def full_copy(i, up):
        n, target = (0, right) if up else (1, left)
        return remote(send_full.at[n, i], recv_full.at[n, i], rs_s.at[3 + n, i], rs_r.at[3 + n, i], target)

    def home_copy(i):
        zt = lax.rem(z + pick(i, REDUCE_ORDER), NZ)
        return remote(send_z.at[i], recv_z.at[i], rs_s.at[5, i], rs_r.at[5, i], dev(x, y, zt, k))

    def chip_sum(i, dest):
        return part[i, dest, k] + pair_in[i, dest]

    def col_part(i):
        shift = pick(i, REDUCE_ORDER)
        zt = lax.rem(z + shift, NZ)
        h = lax.rem(shift + FIRST, 2)
        b = zt // 2
        for q in range(2):
            lanes = slice(q * QUARTER, (q + 1) * QUARTER)
            cell = lax.select(chosen[1] == b, cells[1, h, :, lanes], jnp.zeros((BLOCK, QUARTER), BF16))
            found = lax.dot_general(
                lax.select(chosen[0] == b, cells[0, h, :, lanes], cell),
                rows[...],
                (((0,), (0,)), ((), ())),
                preferred_element_type=F32,
            )
            part[i, 2 * q : 2 * q + 2] = found.reshape(2, NK, PIECE, D)

    def row_part(q):
        at = pl.ds(pl.multiple_of(q * QUARTER, QUARTER), QUARTER)
        result = jnp.zeros((QUARTER, D), F32)
        for s in range(2):
            for h in range(2):
                result = result + jnp.dot(
                    cells[s, h, at], mine[s, h].reshape(HALF, D), preferred_element_type=F32
                )
        return result

    def xhalf(up):
        n, target = (0, east) if up else (1, west)
        return remote(xsend_half.at[n], xrecv_half.at[n], x_s.at[6 + n], x_r.at[6 + n], target)

    def xfull(up):
        n, target = (0, east) if up else (1, west)
        return remote(xsend_full.at[n], xrecv_full.at[n], x_s.at[8 + n], x_r.at[8 + n], target)

    lower = PIECE // 2

    def at_step(t, first, count, work):
        @pl.when((t >= first) & (t < first + count))
        def _():
            work(t - first)

    def gather_z(i):
        zs = lax.rem(z + pick(i, GATHER_ORDER), NZ)

        @pl.when(i != OWN_IN)
        def _():
            z_arrival(zs).wait_recv()
            y_copy(zs, True).start()
            y_copy(zs, False).start()

    def gather_more(i):
        @pl.when(4 + i != OWN_IN)
        def _():
            z_copy(4 + i).start()

    def gather_near(i):
        zs = lax.rem(z + pick(i, GATHER_ORDER), NZ)
        y_arrival(zs, True).wait_recv()
        y_forward(zs, True).start()
        y_arrival(zs, False).wait_recv()
        y_forward(zs, False).start()

    def gather_far(i):
        zs = lax.rem(z + pick(i, GATHER_ORDER), NZ)
        y_far(zs, True).wait_recv()
        y_far(zs, False).wait_recv()
        mate_copy(zs).start()

    def gather_rows(_):
        for j in range(2):
            x_arrival(j).wait_recv()
            x_copy(4 + j).start()

    def half_ready(h):
        for j in range(4):
            mate_arrival(lax.rem(z + GATHER_ORDER[4 * h + j], NZ)).wait_recv()

    def rows_ready(_):
        for j in range(2, 6):
            x_arrival(j).wait_recv()

    def prepare_two(i):
        prepare(2 * i)
        prepare(2 * i + 1)

    def two_tiles(h, n):
        cell_tile(h, 2 * n)
        cell_tile(h, 2 * n + 1)

    def reduce_start(i):
        col_part(i)
        mate_send(i).start()

    def reduce_far(j):
        mate_recv(j).wait_recv()
        value = chip_sum(j, y2).astype(BF16)
        send_half[0, j] = value[:lower]
        half_copy(j, True).start()
        send_half[1, j] = value[lower:]
        half_copy(j, False).start()

    def reduce_near(j):
        half_copy(j, True).wait_recv()
        value = chip_sum(j, yp)
        send_full[0, j, :lower] = (value[:lower] + recv_half[0, j].astype(F32)).astype(BF16)
        send_full[0, j, lower:] = value[lower:].astype(BF16)
        full_copy(j, True).start()
        half_copy(j, False).wait_recv()
        value = chip_sum(j, ym)
        send_full[1, j, :lower] = value[:lower].astype(BF16)
        send_full[1, j, lower:] = (value[lower:] + recv_half[1, j].astype(F32)).astype(BF16)
        full_copy(j, False).start()

    def reduce_home(j):
        full_copy(j, True).wait_recv()
        full_copy(j, False).wait_recv()
        value = chip_sum(j, y) + recv_full[0, j].astype(F32) + recv_full[1, j].astype(F32)

        @pl.when(j == OWN_OUT)
        def _():
            col_grad[...] = value

        @pl.when(j != OWN_OUT)
        def _():
            send_z[j] = value.astype(BF16)
            home_copy(j).start()

    def row_far(_):
        value = row_part(x2).astype(BF16)
        xsend_half[0] = value[:128]
        xsend_half[1] = value[128:]
        xhalf(True).start()
        xhalf(False).start()

    def row_east(_):
        value = row_part(xp)
        xhalf(True).wait_recv()
        xsend_full[0, :128] = (value[:128] + xrecv_half[0].astype(F32)).astype(BF16)
        xsend_full[0, 128:] = value[128:].astype(BF16)
        xfull(True).start()

    def row_west(_):
        value = row_part(xm)
        xhalf(False).wait_recv()
        xsend_full[1, :128] = value[:128].astype(BF16)
        xsend_full[1, 128:] = (value[128:] + xrecv_half[1].astype(F32)).astype(BF16)
        xfull(False).start()

    def row_own(_):
        own_grad[...] = row_part(x)

    def result_copy(i):
        at = pl.ds((0, 2 * QUARTER)[i], (2 * QUARTER, 2 * PIECE)[i])
        return pltpu.make_async_copy(made.at[at], result.at[at], cnt_sem.at[10 + i])

    def row_update(_):
        sums_copy(0).wait()
        xfull(True).wait_recv()
        xfull(False).wait_recv()
        for lane in range(0, D, 128):
            at = slice(lane, lane + 128)
            value = row_local[:, at]
            grad = own_grad[:, at] + xrecv_full[0, :, at].astype(F32) + xrecv_full[1, :, at].astype(F32)
            grad = grad + decay[...] * value
            sums = row_sums[:, at] + grad * grad
            made[:QUARTER, at] = value - learn_rate * grad * lax.rsqrt(sums)
            made[QUARTER : 2 * QUARTER, at] = sums
        result_copy(0).start()

    def step(t, _):
        at_step(t, 0, 8, gather_z)
        at_step(t, GATHER_MORE, 4, gather_more)
        at_step(t, GATHER_NEAR, 8, gather_near)
        at_step(t, GATHER_FAR, 8, gather_far)
        at_step(t, 2, 1, gather_rows)
        at_step(t, REDUCE_HOME, 8, reduce_home)
        at_step(t, REDUCE_NEAR, 8, reduce_near)
        at_step(t, REDUCE_FAR, 8, reduce_far)
        at_step(t, 0, 4, prepare_two)
        at_step(t, CELLS, 1, rows_ready)
        at_step(t, CELLS, 1, lambda _: half_ready(0))
        at_step(t, CELLS, 2, lambda n: two_tiles(0, n))
        at_step(t, CELLS_MORE, 1, lambda _: half_ready(1))
        at_step(t, CELLS_MORE, 2, lambda n: two_tiles(1, n))
        at_step(t, REDUCE, 8, reduce_start)
        at_step(t, ROWS, 1, row_far)
        at_step(t, ROWS + 1, 1, row_east)
        at_step(t, ROWS + 2, 1, row_west)
        at_step(t, ROWS + 3, 1, row_own)
        at_step(t, ROWS + 6, 1, row_update)
        return 0

    lax.fori_loop(0, REDUCE_HOME + 8, step, 0)
    sums_copy(1).wait()
    for j in OTHERS:
        home_copy(j).wait_recv()
    for lane in range(0, D, 128):
        at = slice(lane, lane + 128)
        grad = col_grad[:, at]
        for j in OTHERS:
            grad = grad + recv_z[j, :, at].astype(F32)
        sums = col_sums[:, at] + grad * grad
        made[2 * QUARTER : 2 * QUARTER + PIECE, at] = (
            col_local[:, at] - learn_rate * grad * lax.rsqrt(sums)
        )
        made[2 * QUARTER + PIECE :, at] = sums
    result_copy(1).start()

    for j in range(NZ):
        if j != OWN_IN:
            z_copy(j).wait_send()

    def drain(j, _):
        for up in (True, False):
            y_copy(j, up).wait_send()
            y_forward(j, up).wait_send()
            half_copy(j, up).wait_send()
            full_copy(j, up).wait_send()
        mate_copy(j).wait_send()
        mate_send(j).wait_send()

        @pl.when(j != OWN_OUT)
        def _():
            home_copy(j).wait_send()

        return 0

    lax.fori_loop(0, NZ, drain, 0)
    for j in range(6):
        x_copy(j).wait_send()
    for up in (True, False):
        xhalf(up).wait_send()
        xfull(up).wait_send()
    for i in range(2):
        result_copy(i).wait()


def split_kernel(result, row_new, row_accum_new, col_new, col_accum_new, held, sem):
    reads, writes = [], []
    first = 0
    for i, out in enumerate((row_new, row_accum_new, col_new, col_accum_new)):
        at = pl.ds(first, out.shape[0])
        reads.append(pltpu.make_async_copy(result.at[at], held.at[at], sem.at[i]))
        writes.append(pltpu.make_async_copy(held.at[at], out, sem.at[4 + i]))
        first += out.shape[0]
    for read in reads:
        read.start()
    for read, write in zip(reads, writes):
        read.wait()
        write.start()
    for write in writes:
        write.wait()


def body(
    row_embed,
    row_accum,
    col_embed,
    col_accum,
    col_freq,
    row_freq,
    block_cols,
    counts,
    excluded,
    log_total,
):
    smem = pl.BlockSpec(memory_space=pltpu.SMEM)
    hbm = pl.BlockSpec(memory_space=pl.ANY)
    row_shape = jax.ShapeDtypeStruct((QUARTER, D), F32)
    col_shape = jax.ShapeDtypeStruct((PIECE, D), F32)
    result = pl.pallas_call(
        step_kernel,
        out_shape=jax.ShapeDtypeStruct((2 * QUARTER + 2 * PIECE, D), F32),
        in_specs=[smem, smem] + [hbm] * 8,
        out_specs=hbm,
        scratch_shapes=[
            pltpu.VMEM((QUARTER, D), F32),
            pltpu.VMEM((PIECE, D), F32),
            pltpu.VMEM((1, BLOCK), jnp.int32),
            pltpu.VMEM((1, NY * BLOCK), jnp.int32),
            pltpu.VMEM((1, EXCLUDED), jnp.int32),
            pltpu.VMEM((2 * QUARTER + 2 * PIECE, D), F32),
            pltpu.VMEM((QUARTER, D), F32),
            pltpu.VMEM((PIECE, D), F32),
            pltpu.VMEM((QUARTER, D), F32),
            pltpu.VMEM((PIECE, D), F32),
            pltpu.VMEM((QUARTER, 128), F32),
            pltpu.VMEM((NZ, NY, NK, PIECE, D), BF16),
            pltpu.VMEM((2, 2, 2, QUARTER, D), BF16),
            pltpu.VMEM((BLOCK, D), BF16),
            pltpu.VMEM((2, 2, BLOCK, HALF), jnp.int32),
            pltpu.VMEM((2, 2, BLOCK, HALF), F32),
            pltpu.VMEM((2, 2, BLOCK, HALF), F32),
            pltpu.VMEM((2, 2, BLOCK, HALF), BF16),
            pltpu.VMEM((BLOCK, 128), F32),
            pltpu.VMEM((NZ, NY, NK, PIECE, D), F32),
            pltpu.VMEM((NZ, NY, PIECE, D), F32),
            pltpu.VMEM((2, NZ, PIECE // 2, D), BF16),
            pltpu.VMEM((2, NZ, PIECE // 2, D), BF16),
            pltpu.VMEM((2, NZ, PIECE, D), BF16),
            pltpu.VMEM((2, NZ, PIECE, D), BF16),
            pltpu.VMEM((NZ, PIECE, D), BF16),
            pltpu.VMEM((NZ, PIECE, D), BF16),
            pltpu.VMEM((2, 128, D), BF16),
            pltpu.VMEM((2, 128, D), BF16),
            pltpu.VMEM((2, QUARTER, D), BF16),
            pltpu.VMEM((2, QUARTER, D), BF16),
            pltpu.SemaphoreType.DMA((17,)),
            pltpu.SemaphoreType.DMA((6, NZ)),
            pltpu.SemaphoreType.DMA((6, NZ)),
            pltpu.SemaphoreType.DMA((6, NZ)),
            pltpu.SemaphoreType.DMA((6, NZ)),
            pltpu.SemaphoreType.DMA((10,)),
            pltpu.SemaphoreType.DMA((10,)),
        ],
        compiler_params=pltpu.CompilerParams(
            collective_id=0, has_side_effects=True, vmem_limit_bytes=58 << 20
        ),
        cost_estimate=pl.CostEstimate(
            flops=8 << 30, bytes_accessed=12 << 20, transcendentals=8 << 20
        ),
        name="swivel_step",
    )(
        block_cols.reshape(2),
        log_total.reshape(1),
        row_embed,
        col_embed[0],
        row_freq.reshape(1, BLOCK),
        col_freq,
        excluded.reshape(1, EXCLUDED),
        row_accum,
        col_accum[0],
        counts[0, 0],
    )
    row_new, row_accum_new, col_new, col_accum_new = pl.pallas_call(
        split_kernel,
        out_shape=(row_shape, row_shape, col_shape, col_shape),
        in_specs=[hbm],
        out_specs=(hbm, hbm, hbm, hbm),
        scratch_shapes=[
            pltpu.VMEM((2 * QUARTER + 2 * PIECE, D), F32),
            pltpu.SemaphoreType.DMA((8,)),
        ],
        name="split_result",
    )(result)
    return (row_new, row_accum_new, col_new[None], col_accum_new[None])


def solution(mesh):
    in_specs = (
        P(("row", "col"), None),
        P(("row", "col"), None),
        P("col", "row", None),
        P("col", "row", None),
        P("col", None),
        P("row"),
        P("row", "col", None),
        P("row", "col", None, None, None),
        P(),
        P(),
    )
    out_specs = (
        P(("row", "col"), None),
        P(("row", "col"), None),
        P("col", "row", None),
        P("col", "row", None),
    )
    return jax.shard_map(body, mesh=mesh, in_specs=in_specs, out_specs=out_specs, check_vma=False)
```

profile of v0, /device:TPU:32, one launch (start us, length us, event | category | flops | bytes accessed | tf_op | source)
XLA Modules:
  0.0 70.9 jit_solution(9769241395374961010)
XLA Ops:
  1.3 67.4 %swivel_step.1.result = f32[640,512]{1,0:T(8,128)} custom-call(s32[2]{0:T(128)} %bitcast.17, f32[1]{0:T(128)} %bitcast.9.total, f32[256,512]{1,0:T(8,128)} %row_in.1, f32[64,512]{1,0:T(8,128)} %bitcast.11, s32[1,1024]{1,0:T(1,128)} %bitcast.15, s32[1,4096]{1,0:T(1,128)} %col_freq_in.1, s32[1,512]{1,0:T(1,128)} %bitcast.16, f32[256,512]{1,0:T(8,128)} %row_accum.1, ...), custom_call_target="tpu_custom_call" | custom-call | flops 8589934592 | bytes 12582912 | tf_op jit(solution)/shard_map/swivel_step/pallas_call | solution.py:526
  68.7 2.2 %split_result.1 = (f32[256,512]{1,0:T(8,128)}, f32[256,512]{1,0:T(8,128)}, f32[64,512]{1,0:T(8,128)}, f32[64,512]{1,0:T(8,128)}) custom-call(f32[640,512]{1,0:T(8,128)} %swivel_step.1.result), custom_call_target="tpu_custom_call" | custom-call | tf_op jit(solution)/shard_map/split_result/pallas_call | solution.py:590
where the time goes:
time: 71 us; the launch traced here: 70.9 us
  Pallas kernels  69.6 us (98%)
  between operations  1.29 us (2%)
    pallas_call x1, Pallas kernels, body(): pl.pallas_call(step_kernel, out_shape=jax.ShapeDtypeStruct((2 * QUARTER +...  67.4 us
    pallas_call x1, Pallas kernels, body(): pl.pallas_call(split_kernel, out_shape=(row_shape, row_shape, col_shape,...  2.16 us

commit v1 on v0

--- a/solution.py
+++ b/solution.py
@@ -428,6 +428,7 @@
         at_step(t, GATHER_NEAR, 8, gather_near)
         at_step(t, GATHER_FAR, 8, gather_far)
         at_step(t, 2, 1, gather_rows)
+        at_step(t, REDUCE, 8, reduce_start)
         at_step(t, REDUCE_HOME, 8, reduce_home)
         at_step(t, REDUCE_NEAR, 8, reduce_near)
         at_step(t, REDUCE_FAR, 8, reduce_far)
@@ -437,7 +438,6 @@
         at_step(t, CELLS, 2, lambda n: two_tiles(0, n))
         at_step(t, CELLS_MORE, 1, lambda _: half_ready(1))
         at_step(t, CELLS_MORE, 2, lambda n: two_tiles(1, n))
-        at_step(t, REDUCE, 8, reduce_start)
         at_step(t, ROWS, 1, row_far)
         at_step(t, ROWS + 1, 1, row_east)
         at_step(t, ROWS + 2, 1, row_west)

time: 71 us -> 70.4 us (level)
  no operation moved by 1% of the time
where the time goes in v1:
time: 70.4 us; the launch traced here: 70.3 us
  Pallas kernels  69 us (98%)
  between operations  1.29 us (2%)
    pallas_call x1, Pallas kernels, body(): pl.pallas_call(step_kernel, out_shape=jax.ShapeDtypeStruct((2 * QUARTER +...  66.9 us
    pallas_call x1, Pallas kernels, body(): pl.pallas_call(split_kernel, out_shape=(row_shape, row_shape, col_shape,...  2.16 us

profile of v1, /device:TPU:32, one launch (start us, length us, event | category | flops | bytes accessed | tf_op | source)
XLA Modules:
  0.0 70.3 jit_solution(1630947307034581409)
XLA Ops:
  1.3 66.9 %swivel_step.1.result = f32[640,512]{1,0:T(8,128)} custom-call(s32[2]{0:T(128)} %bitcast.17, f32[1]{0:T(128)} %bitcast.9.total, f32[256,512]{1,0:T(8,128)} %row_in.1, f32[64,512]{1,0:T(8,128)} %bitcast.11, s32[1,1024]{1,0:T(1,128)} %bitcast.15, s32[1,4096]{1,0:T(1,128)} %col_freq_in.1, s32[1,512]{1,0:T(1,128)} %bitcast.16, f32[256,512]{1,0:T(8,128)} %row_accum.1, ...), custom_call_target="tpu_custom_call" | custom-call | flops 8589934592 | bytes 12582912 | tf_op jit(solution)/shard_map/swivel_step/pallas_call | solution.py:526
  68.1 2.2 %split_result.1 = (f32[256,512]{1,0:T(8,128)}, f32[256,512]{1,0:T(8,128)}, f32[64,512]{1,0:T(8,128)}, f32[64,512]{1,0:T(8,128)}) custom-call(f32[640,512]{1,0:T(8,128)} %swivel_step.1.result), custom_call_target="tpu_custom_call" | custom-call | tf_op jit(solution)/shard_map/split_result/pallas_call | solution.py:590

commit v2 on v1

--- a/solution.py
+++ b/solution.py
@@ -425,6 +425,7 @@
     def step(t, _):
         at_step(t, 0, 8, gather_z)
         at_step(t, GATHER_MORE, 4, gather_more)
+        at_step(t, 0, 4, prepare_two)
         at_step(t, GATHER_NEAR, 8, gather_near)
         at_step(t, GATHER_FAR, 8, gather_far)
         at_step(t, 2, 1, gather_rows)
@@ -432,7 +433,6 @@
         at_step(t, REDUCE_HOME, 8, reduce_home)
         at_step(t, REDUCE_NEAR, 8, reduce_near)
         at_step(t, REDUCE_FAR, 8, reduce_far)
-        at_step(t, 0, 4, prepare_two)
         at_step(t, CELLS, 1, rows_ready)
         at_step(t, CELLS, 1, lambda _: half_ready(0))
         at_step(t, CELLS, 2, lambda n: two_tiles(0, n))

time: 70.4 us -> 70.6 us (level)
  the two profiles are of different devices: /device:TPU:32 before, /device:TPU:8 now
where the time goes in v2:
time: 70.6 us; the launch traced here: 70.5 us
  Pallas kernels  69.2 us (98%)
  between operations  1.29 us (2%)
    pallas_call x1, Pallas kernels, body(): pl.pallas_call(step_kernel, out_shape=jax.ShapeDtypeStruct((2 * QUARTER +...  67 us
    pallas_call x1, Pallas kernels, body(): pl.pallas_call(split_kernel, out_shape=(row_shape, row_shape, col_shape,...  2.16 us

profile of v2, /device:TPU:8, one launch (start us, length us, event | category | flops | bytes accessed | tf_op | source)
XLA Modules:
  0.0 70.5 jit_solution(2606892550035197653)
XLA Ops:
  1.3 67.0 %swivel_step.1.result = f32[640,512]{1,0:T(8,128)} custom-call(s32[2]{0:T(128)} %bitcast.17, f32[1]{0:T(128)} %bitcast.9.total, f32[256,512]{1,0:T(8,128)} %row_in.1, f32[64,512]{1,0:T(8,128)} %bitcast.11, s32[1,1024]{1,0:T(1,128)} %bitcast.15, s32[1,4096]{1,0:T(1,128)} %col_freq_in.1, s32[1,512]{1,0:T(1,128)} %bitcast.16, f32[256,512]{1,0:T(8,128)} %row_accum.1, ...), custom_call_target="tpu_custom_call" | custom-call | flops 8589934592 | bytes 12582912 | tf_op jit(solution)/shard_map/swivel_step/pallas_call | solution.py:526
  68.3 2.2 %split_result.1 = (f32[256,512]{1,0:T(8,128)}, f32[256,512]{1,0:T(8,128)}, f32[64,512]{1,0:T(8,128)}, f32[64,512]{1,0:T(8,128)}) custom-call(f32[640,512]{1,0:T(8,128)} %swivel_step.1.result), custom_call_target="tpu_custom_call" | custom-call | tf_op jit(solution)/shard_map/split_result/pallas_call | solution.py:590
